TPU v7x, 32 devices: a whole 2x2x4 slice. The times are simulated.
32 devices in a mesh: blk: 8 (over y, x, core), tm: 4 (over z).
Axes of the slice: x: 2, y: 2, z: 4, core: 2. Of those that a mesh axis runs over, the one named last changes fastest.
Arguments:
- records: bfloat16 [2048, 16, 512], P('blk', 'tm'), may hold values from -6 to 6
- glitch_mask: int32 [2048, 16], P('blk'), may hold values 0 or 1
- fir_taps: bfloat16 [65], replicated, may hold values from -1.1953125 to 1.1953125
Outputs:
- correlations: bfloat16 [16, 2048, 2048], P('tm', 'blk')
All inputs are finite; a program needn't handle non-finite values. No bound on the sum of `glitch_mask` on one device may be relied on, other than what follows from the above.
Results may differ from a plain program's by a relative error of at most 0.015.
Values may be sent and summed in bfloat16 or wider, within the bound.
A program may use at most 256 MiB of HBM per device.

v0:
```python
import math

import jax
import jax.numpy as jnp
import numpy as np
from jax import lax
from jax.experimental import pallas as pl
from jax.experimental.pallas import tpu as pltpu
from jax.sharding import PartitionSpec as P

BINS = 128
FIRST_BIN = 16
SMOOTH = 64
LAGS = 16
GROUP = 4


def dft_thirds(seglen):
    sample = np.arange(seglen)[:, None]
    freq = np.arange(BINS)[None, :] + FIRST_BIN
    angle = (sample * freq % seglen) * (2.0 * math.pi / seglen)
    rest = np.concatenate([np.cos(angle), -np.sin(angle)], axis=1).astype(np.float32)
    thirds = []
    for _ in range(3):
        part = rest.astype(jnp.bfloat16)
        thirds.append(part)
        rest = rest - part.astype(np.float32)
    return np.concatenate(thirds, axis=1)


def lag_rows(seg_total, seglen):
    delay = np.arange(LAGS)[:, None] - LAGS // 2
    freq = np.arange(BINS)[None, :] + FIRST_BIN
    angle = (delay * freq % seglen) * (2.0 * math.pi / seglen)
    factor = 1.0 / math.sqrt(seg_total * BINS)
    tables = np.stack([np.cos(angle), np.sin(angle)]).astype(np.float32) * np.float32(factor)
    return tables.astype(jnp.bfloat16).astype(np.float32)


def filter_matrix(fir_taps, seglen):
    half = (fir_taps.shape[0] - 1) // 2
    period = 2 * seglen
    line = jnp.pad(fir_taps[::-1], (seglen - 1 - half, seglen - half))
    rows = jnp.tile(line, seglen)[: seglen * (period - 1)].reshape(seglen, period - 1)
    return rows[:, seglen - 1 :]


def transform_table(fir_taps, seglen):
    parts = jnp.dot(
        filter_matrix(fir_taps, seglen),
        jnp.asarray(dft_thirds(seglen)),
        preferred_element_type=jnp.float32,
    )
    width = 2 * BINS
    total = parts[:, :width] + (parts[:, width : 2 * width] + parts[:, 2 * width :])
    return total.astype(jnp.bfloat16)


def whiten(samples, usable, fir_taps):
    seglen = samples.shape[1]
    source = lax.broadcasted_iota(jnp.int32, (seglen, seglen), 0)
    target = lax.broadcasted_iota(jnp.int32, (seglen, seglen), 1)
    band_ones = jnp.where(jnp.abs(source - target) <= SMOOTH, 1.0, 0.0).astype(jnp.bfloat16)
    where = lax.broadcasted_iota(jnp.int32, (1, seglen), 1)
    counts = jnp.minimum(where, SMOOTH) + jnp.minimum(seglen - 1 - where, SMOOTH) + 1
    envelope = jnp.dot(
        jnp.abs(samples), band_ones, preferred_element_type=jnp.float32
    ) / counts.astype(jnp.float32)
    normal = (samples.astype(jnp.float32) / (envelope + 1e-06)).astype(jnp.bfloat16)
    spectra = jnp.dot(normal, transform_table(fir_taps, seglen), preferred_element_type=jnp.float32)
    power = jnp.sum(spectra * spectra, axis=1, keepdims=True) * jnp.float32(1.0 / BINS)
    scale = usable.astype(jnp.float32)[:, None] / jnp.sqrt(power + 1e-06)
    return (spectra * scale).astype(jnp.bfloat16)


def gathered_body(records, glitch_mask, fir_taps):
    tm_count = lax.axis_size("tm")
    tm_index = lax.axis_index("tm")
    chans, segs, seglen = records.shape
    seg_total = glitch_mask.shape[1]
    usable = lax.dynamic_slice_in_dim(glitch_mask, tm_index * segs, segs, 1)
    white = whiten(records.reshape(chans * segs, seglen), usable.reshape(chans * segs), fir_taps)
    slab = white.reshape(chans, segs * 2 * BINS)
    column = lax.all_gather(slab, "tm", axis=1, tiled=True)
    every = lax.all_gather(column, "blk", axis=0, tiled=True)
    lags_dev = LAGS // tm_count
    tables = lax.dynamic_slice_in_dim(
        jnp.asarray(lag_rows(seg_total, seglen)), tm_index * lags_dev, lags_dev, 1
    )
    cos_rows = tables[0][:, None, None, :]
    sin_rows = tables[1][:, None, None, :]
    own = column.reshape(chans, seg_total, 2, BINS).astype(jnp.float32)
    real_part, imag_part = own[None, :, :, 0], own[None, :, :, 1]
    turned = jnp.stack(
        [cos_rows * real_part - sin_rows * imag_part, cos_rows * imag_part + sin_rows * real_part],
        axis=3,
    ).astype(jnp.bfloat16)
    left = turned.reshape(lags_dev, chans, seg_total * 2 * BINS)
    return jnp.einsum("lik,jk->lij", left, every, preferred_element_type=jnp.float32).astype(
        jnp.bfloat16
    )


NEAREST = ((0, 1, 2, 3), (1, 2, 0, 3), (2, 1, 3, 0), (3, 2, 1, 0))
MESH = pl.DeviceIdType.MESH


def kernel(x_ref, use_ref, line_ref, dft_ref, tab_ref, out_ref, slabs, left, acc, done, sent, got, outs):
    segs, chans, seglen = x_ref.shape
    width = 2 * BINS
    depth = segs * width
    lags = left.shape[1]
    half = chans // 2
    b, z = lax.axis_index("blk"), lax.axis_index("tm")
    core = lax.rem(b, 2)
    at_x = lax.rem(lax.div(b, 2), 2)
    at_y = lax.div(b, 4)
    sib = b + 1 - 2 * core
    by_x = b + 2 - 4 * at_x
    by_y = b + 4 - 8 * at_y
    across = by_x + 4 - 8 * at_y
    up, down = z + 1, z - 1
    has_up, has_down = z < 3, z > 0

    barrier = pltpu.get_barrier_semaphore()
    for peer in (sib, by_x, by_y):
        pl.semaphore_signal(barrier, inc=1, device_id=(peer, z), device_id_type=MESH)

    @pl.when(has_up)
    def _():
        pl.semaphore_signal(barrier, inc=1, device_id=(b, up), device_id_type=MESH)

    @pl.when(has_down)
    def _():
        pl.semaphore_signal(barrier, inc=1, device_id=(b, down), device_id_type=MESH)

    def slab_of(plane, block):
        return plane * 8 + block

    own = slab_of(z, b)
    line = jnp.broadcast_to(line_ref[...], (seglen, 2 * seglen))
    fir = pltpu.roll(line, 0, 1, stride=1, stride_axis=0)[:, :seglen].astype(jnp.bfloat16)
    parts = jnp.dot(fir, dft_ref[...], preferred_element_type=jnp.float32)
    table = (parts[:, :width] + (parts[:, width : 2 * width] + parts[:, 2 * width :])).astype(jnp.bfloat16)
    source = lax.broadcasted_iota(jnp.int32, (seglen, seglen), 0)
    target = lax.broadcasted_iota(jnp.int32, (seglen, seglen), 1)
    band_ones = jnp.where(jnp.abs(source - target) <= SMOOTH, 1.0, 0.0).astype(jnp.bfloat16)
    where = lax.broadcasted_iota(jnp.int32, (1, seglen), 1)
    counts = jnp.minimum(where, SMOOTH) + jnp.minimum(seglen - 1 - where, SMOOTH) + 1
    counts = counts.astype(jnp.float32)
    def whiten_segment(s):
        samples = x_ref[s]
        envelope = jnp.dot(jnp.abs(samples), band_ones, preferred_element_type=jnp.float32) / counts
        normal = (samples.astype(jnp.float32) / (envelope + 1e-06)).astype(jnp.bfloat16)
        spectra = jnp.dot(normal, table, preferred_element_type=jnp.float32)
        power = jnp.sum(spectra * spectra, axis=1, keepdims=True) * jnp.float32(1.0 / BINS)
        scale = use_ref[:, s : s + 1] / jnp.sqrt(power + 1e-06)
        slabs[own, :, s * width : (s + 1) * width] = (spectra * scale).astype(jnp.bfloat16)

    sends = {}

    def view(slab, part):
        if part is None:
            return slabs.at[slab], got.at[slab, 0]
        if part >= 2:
            columns = pl.ds((part - 2) * depth // 2, depth // 2)
            return slabs.at[slab, :, columns], got.at[slab, 0]
        return slabs.at[slab, pl.ds(part * half, half)], got.at[slab, part]

    def make(index, slab, block, plane, part):
        ref, sem = view(slab, part)
        return pltpu.make_async_remote_copy(
            src_ref=ref, dst_ref=ref, send_sem=sent.at[index], recv_sem=sem,
            device_id=(block, plane), device_id_type=MESH,
        )

    def send(name, slab, block, plane, part=None, when=None):
        if name not in sends:
            sends[name] = (len(sends), slab, block, plane, part, when)
        go = make(*sends[name][:-1]).start
        if when is None:
            go()
        else:
            pl.when(when)(go)

    def arrive(slab, part=None):
        make(0, slab, sib, z, part).wait_recv()

    plane_at, onward, goes_on = [z], [None], [None]
    for step in range(1, 4):
        plane = sum(jnp.where(z == at, NEAREST[at][step], 0) for at in range(4))
        following = jnp.where(plane > z, z - 1, z + 1)
        plane_at.append(plane)
        onward.append(following)
        goes_on.append(jnp.logical_and(following >= 0, following <= 3))

    def turn(step):
        slab = slab_of(plane_at[step], b)

        def one(lag, carry):
            row = z * lags + lag
            cos_row = tab_ref[0, pl.ds(row, 1), :]
            sin_row = tab_ref[1, pl.ds(row, 1), :]
            for s in range(segs):
                at = s * width
                real_part = slabs[slab, :, at : at + BINS].astype(jnp.float32)
                imag_part = slabs[slab, :, at + BINS : at + width].astype(jnp.float32)
                left[step, lag, :, at : at + BINS] = (
                    cos_row * real_part - sin_row * imag_part
                ).astype(jnp.bfloat16)
                left[step, lag, :, at + BINS : at + width] = (
                    cos_row * imag_part + sin_row * real_part
                ).astype(jnp.bfloat16)
            return carry

        lax.fori_loop(0, lags, one, 0)

    copies = []

    def correlate(step, block):
        pair = lax.div(block, 2)
        first_slab = slab_of(plane_at[step], pair * 2)
        columns = pl.ds(pl.multiple_of(pair * 2 * chans, 2 * chans), 2 * chans)

        right = slabs[pl.ds(first_slab, 2)].reshape(2 * chans, depth)

        def one(at, carry):
            some = pl.ds(at * GROUP, GROUP)
            term = lax.dot_general(
                left[step, some].reshape(GROUP * chans, depth),
                right,
                (((1,), (1,)), ((), ())),
                preferred_element_type=jnp.float32,
            ).reshape(GROUP, chans, 2 * chans)
            if step == 0:
                acc[some, :, columns] = term
            elif step < 3:
                acc[some, :, columns] += term
            else:
                done[some, :, columns] = (acc[some, :, columns] + term).astype(jnp.bfloat16)
            return carry

        lax.fori_loop(0, lags // GROUP, one, 0)
        if step == 3:
            copy = pltpu.make_async_copy(
                done.at[:, :, columns], out_ref.at[:, :, columns], outs.at[len(copies)]
            )
            copy.start()
            copies.append(copy)

    def other_core(block):
        return block + 1 - 2 * core

    in_middle = jnp.logical_and(has_up, has_down)
    at_end = jnp.logical_not(in_middle)
    mine, xs, ys, corners = [
        [slab_of(plane, block) for plane in plane_at] for block in (b, by_x, by_y, across)
    ]
    twins = {
        key: [slab_of(plane, other_core(block)) for plane in plane_at]
        for key, block in (("b", b), ("x", by_x), ("y", by_y), ("c", across))
    }

    def guarded(when, action):
        if when is None:
            action()
        else:
            pl.when(when)(action)

    def along_z(step, when=None):
        def action():
            slab = mine[step]
            arrive(slab)
            send(("z", step), slab, b, onward[step], when=goes_on[step])
            send(("x", step), slab, by_x, z)
            send(("y", step), slab, by_y, z)
            send(("s", step), slab, sib, z)

        guarded(when, action)

    def neighbours(step):
        arrive(xs[step])
        if step in (0, 3):
            send(("xy", step), xs[step], by_y, z, part=0)
        send(("xs", step), xs[step], sib, z)
        arrive(ys[step])
        if step in (0, 3):
            send(("yx", step), ys[step], by_x, z, part=1)
        send(("ys", step), ys[step], sib, z)

    def corner(step, when=None):
        def action():
            slab = corners[step]
            if step in (0, 3):
                arrive(slab, 0)
                arrive(slab, 1)
            else:
                arrive(slab)
            if step == 0:
                send(("cu",), slab, b, up, when=has_up)
                send(("cd",), slab, b, down, when=has_down)
            elif step == 1:
                send(("cz",), slab, b, onward[1], when=goes_on[1])
            send(("cs", step), slab, sib, z)

        guarded(when, action)

    def multiply(step, keys):
        for key in keys:
            arrive(twins[key][step])
            correlate(step, {"b": b, "x": by_x, "y": by_y, "c": across}[key])

    for part in range(2):
        for segment in range(part * segs // 2, (part + 1) * segs // 2):
            whiten_segment(segment)
        if part == 0:
            pl.semaphore_wait(barrier, 3 + has_up.astype(jnp.int32) + has_down.astype(jnp.int32))
        early = 2 + part
        send(("u", part), own, b, up, early, has_up)
        send(("d", part), own, b, down, early, has_down)
        send(("x", 0, part), own, by_x, z, early)
        send(("y", 0, part), own, by_y, z, early)
        send(("s", 0, part), own, sib, z, early)
    turn(0)
    multiply(0, "b")
    along_z(1)
    along_z(2, in_middle)
    neighbours(0)
    turn(1)
    multiply(0, "xy")
    multiply(1, "b")
    along_z(2, at_end)
    along_z(3, in_middle)
    corner(0)
    turn(2)
    multiply(0, "c")
    neighbours(1)
    along_z(3, at_end)
    corner(1, in_middle)
    multiply(1, "xy")
    multiply(2, "b")
    neighbours(2)
    turn(3)
    multiply(2, "xy")
    multiply(3, "b")
    corner(1, at_end)
    multiply(1, "c")
    neighbours(3)
    multiply(3, "xy")
    corner(2)
    multiply(2, "c")
    corner(3)
    multiply(3, "c")

    for copy in copies:
        copy.wait()
    for index, slab, block, plane, part, when in sends.values():
        guarded(when, make(index, slab, block, plane, part).wait_send)


def kernel_body(records, glitch_mask, fir_taps):
    blocks, planes = lax.axis_size("blk"), lax.axis_size("tm")
    tm_index = lax.axis_index("tm")
    chans, segs, seglen = records.shape
    seg_total = glitch_mask.shape[1]
    lags_dev = LAGS // planes
    depth = segs * 2 * BINS
    usable = lax.dynamic_slice_in_dim(glitch_mask, tm_index * segs, segs, 1).astype(jnp.float32)
    middle = (fir_taps.shape[0] - 1) // 2
    back = fir_taps[::-1].astype(jnp.float32)
    line = jnp.concatenate(
        [back[middle:], jnp.zeros((2 * seglen - 2 * middle - 1,), jnp.float32), back[:middle]]
    )[None, :]
    bf16 = jnp.bfloat16
    return pl.pallas_call(
        kernel,
        out_shape=jax.ShapeDtypeStruct((lags_dev, chans, chans * blocks), bf16),
        in_specs=[pl.BlockSpec(memory_space=pltpu.VMEM)] * 5,
        out_specs=pl.BlockSpec(memory_space=pl.ANY),
        scratch_shapes=[
            pltpu.VMEM((blocks * planes, chans, depth), bf16),
            pltpu.VMEM((planes, lags_dev, chans, depth), bf16),
            pltpu.VMEM((lags_dev, chans, chans * blocks), jnp.float32),
            pltpu.VMEM((lags_dev, chans, chans * blocks), bf16),
            pltpu.SemaphoreType.DMA((48,)),
            pltpu.SemaphoreType.DMA((blocks * planes, 2)),
            pltpu.SemaphoreType.DMA((4,)),
        ],
        compiler_params=pltpu.CompilerParams(
            collective_id=0, has_side_effects=True, vmem_limit_bytes=58 * 1024 * 1024
        ),
        cost_estimate=pl.CostEstimate(
            flops=2 * lags_dev * chans * chans * blocks * planes * depth,
            bytes_accessed=2 * lags_dev * chans * chans * blocks,
            transcendentals=0,
        ),
    )(
        jnp.transpose(records, (1, 0, 2)),
        usable,
        line,
        jnp.asarray(dft_thirds(seglen)),
        jnp.asarray(lag_rows(seg_total, seglen)),
    )


def solution(mesh):
    placed = (P("blk", "tm", None), P("blk", None), P())
    small = mesh.shape["blk"] == 8 and mesh.shape["tm"] == 4
    return jax.shard_map(
        kernel_body if small else gathered_body,
        mesh=mesh,
        in_specs=placed,
        out_specs=P("tm", "blk", None),
        check_vma=False,
    )
```

profile of v0, /device:TPU:17, one launch (start us, length us, event | category | flops | bytes accessed | tf_op | source)
XLA Modules:
  0.0 91.0 jit_solution(6710090734335182600)
XLA Ops:
  0.0 0.0 copy-start
  0.0 0.8 rev.3
  0.8 0.1 slice.6
  0.8 0.0 copy-done
  0.9 0.7 pad_maximum_fusion
  1.5 0.1 copy.8
  1.7 0.7 convert_element_type.6.use_ref
  2.3 2.4 %copy.10 = bf16[256,4,512]{2,0,1:T(8,128)(2,1)} copy(bf16[256,4,512]{2,1,0:T(4,128)(2,1)} %param.5) | data formatting | bytes 2097152 | tf_op args[0]
  4.7 81.5 %shard_map.55 = bf16[4,256,2048]{2,1,0:T(8,128)(2,1)} custom-call(bf16[4,256,512]{2,1,0:T(8,128)(2,1)} %bitcast.4, f32[256,4]{1,0:T(8,128)} %convert_element_type.6.use_ref, f32[1,1024]{1,0:T(1,128)} %bitcast.5, bf16[512,768]{1,0:T(8,128)(2,1)} %constant.16.clone.dft_ref, f32[2,16,128]{2,1,0:T(8,128)} %constant.17.clone.tab_ref), custom_call_target="tpu_custom_call" | custom-call | flops 17179869184 | bytes 4194304 | tf_op jit(solution)/shard_map/pallas_call | solution.py:375
  86.3 4.8 %copy.12 = bf16[4,256,2048]{2,1,0:T(8,128)(2,1)} copy(bf16[4,256,2048]{2,1,0:T(8,128)(2,1)} %shard_map.55) | data formatting | bytes 8388608
  (3 shorter events, 0.0 us)
Async XLA Ops:
  0.0 0.8 copy-start
where the time goes:
time: 91.3 us; the launch traced here: 91 us
  Pallas kernels  81.5 us (89%)
  local copies, waits for them, and re-layouts  8.16 us (9%)
  other arithmetic  1.34 us (1%)
    pallas_call x1, Pallas kernels, kernel_body(): pl.pallas_call(kernel, out_shape=jax.ShapeDtypeStruct((lags_dev, chans, c...  81.5 us
    unnamed x5, local copies, waits for them, and re-layouts  7.31 us

commit v1 on v0

v1 whole, which is shorter than its diff:
```python
import math

import jax
import jax.numpy as jnp
import numpy as np
from jax import lax
from jax.experimental import pallas as pl
from jax.experimental.pallas import tpu as pltpu
from jax.sharding import PartitionSpec as P

BINS = 128
FIRST_BIN = 16
SMOOTH = 64
LAGS = 16


def dft_thirds(seglen):
    sample = np.arange(seglen)[:, None]
    freq = np.arange(BINS)[None, :] + FIRST_BIN
    angle = (sample * freq % seglen) * (2.0 * math.pi / seglen)
    rest = np.concatenate([np.cos(angle), -np.sin(angle)], axis=1).astype(np.float32)
    thirds = []
    for _ in range(3):
        part = rest.astype(jnp.bfloat16)
        thirds.append(part)
        rest = rest - part.astype(np.float32)
    return np.concatenate(thirds, axis=1)


def lag_rows(seg_total, seglen):
    delay = np.arange(LAGS)[:, None] - LAGS // 2
    freq = np.arange(BINS)[None, :] + FIRST_BIN
    angle = (delay * freq % seglen) * (2.0 * math.pi / seglen)
    factor = 1.0 / math.sqrt(seg_total * BINS)
    tables = np.stack([np.cos(angle), np.sin(angle)]).astype(np.float32) * np.float32(factor)
    return tables.astype(jnp.bfloat16).astype(np.float32)


def filter_matrix(fir_taps, seglen):
    half = (fir_taps.shape[0] - 1) // 2
    period = 2 * seglen
    line = jnp.pad(fir_taps[::-1], (seglen - 1 - half, seglen - half))
    rows = jnp.tile(line, seglen)[: seglen * (period - 1)].reshape(seglen, period - 1)
    return rows[:, seglen - 1 :]


def transform_table(fir_taps, seglen):
    parts = jnp.dot(
        filter_matrix(fir_taps, seglen),
        jnp.asarray(dft_thirds(seglen)),
        preferred_element_type=jnp.float32,
    )
    width = 2 * BINS
    total = parts[:, :width] + (parts[:, width : 2 * width] + parts[:, 2 * width :])
    return total.astype(jnp.bfloat16)


def whiten(samples, usable, fir_taps):
    seglen = samples.shape[1]
    source = lax.broadcasted_iota(jnp.int32, (seglen, seglen), 0)
    target = lax.broadcasted_iota(jnp.int32, (seglen, seglen), 1)
    band_ones = jnp.where(jnp.abs(source - target) <= SMOOTH, 1.0, 0.0).astype(jnp.bfloat16)
    where = lax.broadcasted_iota(jnp.int32, (1, seglen), 1)
    counts = jnp.minimum(where, SMOOTH) + jnp.minimum(seglen - 1 - where, SMOOTH) + 1
    envelope = jnp.dot(
        jnp.abs(samples), band_ones, preferred_element_type=jnp.float32
    ) / counts.astype(jnp.float32)
    normal = (samples.astype(jnp.float32) / (envelope + 1e-06)).astype(jnp.bfloat16)
    spectra = jnp.dot(normal, transform_table(fir_taps, seglen), preferred_element_type=jnp.float32)
    power = jnp.sum(spectra * spectra, axis=1, keepdims=True) * jnp.float32(1.0 / BINS)
    scale = usable.astype(jnp.float32)[:, None] / jnp.sqrt(power + 1e-06)
    return (spectra * scale).astype(jnp.bfloat16)


def gathered_body(records, glitch_mask, fir_taps):
    tm_count = lax.axis_size("tm")
    tm_index = lax.axis_index("tm")
    chans, segs, seglen = records.shape
    seg_total = glitch_mask.shape[1]
    usable = lax.dynamic_slice_in_dim(glitch_mask, tm_index * segs, segs, 1)
    white = whiten(records.reshape(chans * segs, seglen), usable.reshape(chans * segs), fir_taps)
    slab = white.reshape(chans, segs * 2 * BINS)
    column = lax.all_gather(slab, "tm", axis=1, tiled=True)
    every = lax.all_gather(column, "blk", axis=0, tiled=True)
    lags_dev = LAGS // tm_count
    tables = lax.dynamic_slice_in_dim(
        jnp.asarray(lag_rows(seg_total, seglen)), tm_index * lags_dev, lags_dev, 1
    )
    cos_rows = tables[0][:, None, None, :]
    sin_rows = tables[1][:, None, None, :]
    own = column.reshape(chans, seg_total, 2, BINS).astype(jnp.float32)
    real_part, imag_part = own[None, :, :, 0], own[None, :, :, 1]
    turned = jnp.stack(
        [cos_rows * real_part - sin_rows * imag_part, cos_rows * imag_part + sin_rows * real_part],
        axis=3,
    ).astype(jnp.bfloat16)
    left = turned.reshape(lags_dev, chans, seg_total * 2 * BINS)
    return jnp.einsum("lik,jk->lij", left, every, preferred_element_type=jnp.float32).astype(
        jnp.bfloat16
    )


NEAREST = ((0, 1, 2, 3), (1, 2, 0, 3), (2, 1, 3, 0), (3, 2, 1, 0))
MESH = pl.DeviceIdType.MESH


def kernel(x_ref, use_ref, tap_ref, dft_ref, tab_ref, done, slabs, left, acc, taps, sent, got):
    chans, segs, seglen = x_ref.shape
    width = 2 * BINS
    depth = segs * width
    lags = left.shape[1]
    half = chans // 2
    part_ch = half // 2
    b, z = lax.axis_index("blk"), lax.axis_index("tm")
    core = lax.rem(b, 2)
    at_x = lax.rem(lax.div(b, 2), 2)
    at_y = lax.div(b, 4)
    sib = b + 1 - 2 * core
    by_x = b + 2 - 4 * at_x
    by_y = b + 4 - 8 * at_y
    across = by_x + 4 - 8 * at_y
    up, down = z + 1, z - 1
    has_up, has_down = z < 3, z > 0
    in_middle = jnp.logical_and(has_up, has_down)
    at_end = jnp.logical_not(in_middle)

    def guarded(when, action):
        if when is None:
            action()
        else:
            pl.when(when)(action)

    barrier = pltpu.get_barrier_semaphore()
    for block, plane, when in (
        (sib, z, None), (by_x, z, None), (by_y, z, None), (b, up, has_up), (b, down, has_down)
    ):
        guarded(
            when,
            lambda block=block, plane=plane: pl.semaphore_signal(
                barrier, inc=1, device_id=(block, plane), device_id_type=MESH
            ),
        )

    def slab_of(plane, block):
        return plane * 8 + block

    own = slab_of(z, b)
    taps[...] = jnp.zeros_like(taps)
    taps[0:1, : tap_ref.shape[1]] = tap_ref[...].astype(jnp.float32)
    middle = (tap_ref.shape[1] - 1) // 2
    period = 2 * seglen
    tap_at = lax.broadcasted_iota(jnp.int32, (128, period), 0)
    spot = lax.broadcasted_iota(jnp.int32, (128, period), 1)
    offset = middle - tap_at
    place = jnp.where(spot == jnp.where(offset < 0, offset + period, offset), 1.0, 0.0)
    line = jnp.dot(
        taps[...].astype(jnp.bfloat16), place.astype(jnp.bfloat16), preferred_element_type=jnp.float32
    )[0:1]
    line = jnp.broadcast_to(line, (seglen, period))
    fir = pltpu.roll(line, 0, 1, stride=1, stride_axis=0)[:, :seglen].astype(jnp.bfloat16)
    parts = jnp.dot(fir, dft_ref[...], preferred_element_type=jnp.float32)
    table = (parts[:, :width] + (parts[:, width : 2 * width] + parts[:, 2 * width :])).astype(jnp.bfloat16)
    source = lax.broadcasted_iota(jnp.int32, (seglen, seglen), 0)
    target = lax.broadcasted_iota(jnp.int32, (seglen, seglen), 1)
    band_ones = jnp.where(jnp.abs(source - target) <= SMOOTH, 1.0, 0.0).astype(jnp.bfloat16)
    where = lax.broadcasted_iota(jnp.int32, (1, seglen), 1)
    counts = jnp.minimum(where, SMOOTH) + jnp.minimum(seglen - 1 - where, SMOOTH) + 1
    counts = counts.astype(jnp.float32)
    rows = part_ch * segs
    to_row = lax.broadcasted_iota(jnp.int32, (rows, rows), 0)
    from_row = lax.broadcasted_iota(jnp.int32, (rows, rows), 1)
    by_segment = jnp.where(
        from_row == lax.rem(to_row, part_ch) * segs + lax.div(to_row, part_ch), 1.0, 0.0
    ).astype(jnp.bfloat16)
    wanted = lax.broadcasted_iota(jnp.int32, (use_ref.shape[0], segs * BINS), 0)
    column = lax.div(lax.broadcasted_iota(jnp.int32, (use_ref.shape[0], segs * BINS), 1), BINS)
    usable = lax.dot_general(
        use_ref[...].astype(jnp.bfloat16),
        jnp.where(wanted == z * segs + column, 1.0, 0.0).astype(jnp.bfloat16),
        (((0,), (0,)), ((), ())),
        preferred_element_type=jnp.float32,
    )

    def whiten_half(h):
        samples = x_ref[h * half : (h + 1) * half].reshape(half * segs, seglen)
        envelope = jnp.dot(jnp.abs(samples), band_ones, preferred_element_type=jnp.float32) / counts
        normal = (samples.astype(jnp.float32) / (envelope + 1e-06)).astype(jnp.bfloat16)
        spectra = jnp.dot(normal, table, preferred_element_type=jnp.float32)
        power = jnp.sum(spectra * spectra, axis=1, keepdims=True) * jnp.float32(1.0 / BINS)
        white = (spectra / jnp.sqrt(power + 1e-06)).astype(jnp.bfloat16)
        for k in range(2):
            sorted_rows = jnp.dot(
                by_segment, white[k * rows : (k + 1) * rows], preferred_element_type=jnp.float32
            )
            first = h * half + k * part_ch
            for s in range(segs):
                slabs[own, first : first + part_ch, s * width : (s + 1) * width] = (
                    sorted_rows[s * part_ch : (s + 1) * part_ch]
                    * usable[first : first + part_ch, s * BINS : s * BINS + 1]
                ).astype(jnp.bfloat16)

    sends = {}

    def make(index, slab, block, plane, h):
        ref = slabs.at[slab, pl.ds(h * half, half)]
        return pltpu.make_async_remote_copy(
            src_ref=ref, dst_ref=ref, send_sem=sent.at[index], recv_sem=got.at[slab, h],
            device_id=(block, plane), device_id_type=MESH,
        )

    def send(name, slab, block, plane, h, when=None):
        name = name + (h,)
        if name not in sends:
            sends[name] = (len(sends), slab, block, plane, h, when)
        guarded(when, lambda: make(*sends[name][:-1]).start())

    def arrive(slab, h):
        make(0, slab, sib, z, h).wait_recv()

    plane_at, onward, goes_on = [z], [None], [None]
    for step in range(1, 4):
        plane = sum(jnp.where(z == at, NEAREST[at][step], 0) for at in range(4))
        following = jnp.where(plane > z, z - 1, z + 1)
        plane_at.append(plane)
        onward.append(following)
        goes_on.append(jnp.logical_and(following >= 0, following <= 3))

    def turn(step):
        slab = slab_of(plane_at[step], b)

        def one(lag, carry):
            row = z * lags + lag
            cos_row = tab_ref[0, pl.ds(row, 1), :]
            sin_row = tab_ref[1, pl.ds(row, 1), :]
            for s in range(segs):
                at = s * width
                real_part = slabs[slab, :, at : at + BINS].astype(jnp.float32)
                imag_part = slabs[slab, :, at + BINS : at + width].astype(jnp.float32)
                left[step, lag, :, at : at + BINS] = (
                    cos_row * real_part - sin_row * imag_part
                ).astype(jnp.bfloat16)
                left[step, lag, :, at + BINS : at + width] = (
                    cos_row * imag_part + sin_row * real_part
                ).astype(jnp.bfloat16)
            return carry

        lax.fori_loop(0, lags, one, 0)

    blocks = {"b": b, "x": by_x, "y": by_y, "c": across}
    steps_done = {}

    def multiply(step, key, h):
        block = blocks[key]
        other = block + 1 - 2 * core
        arrive(slab_of(plane_at[step], other), h)
        count = steps_done.get((key, h), 0)
        steps_done[key, h] = count + 1
        pair = lax.div(block, 2) * 2
        right = slabs[pl.ds(slab_of(plane_at[step], pair), 2), h * half : (h + 1) * half]
        term = lax.dot_general(
            left[step].reshape(lags * chans, depth),
            right.reshape(2 * half, depth),
            (((1,), (1,)), ((), ())),
            preferred_element_type=jnp.float32,
        ).reshape(lags, chans, 2 * half)
        at = "bxyc".index(key) * 2 + h
        if count == 0:
            acc[at] = term
        elif count < 3:
            acc[at] += term
        else:
            total = (acc[at] + term).astype(jnp.bfloat16)
            for twin in range(2):
                first = pl.multiple_of((pair + twin) * chans + h * half, half)
                done[:, :, pl.ds(first, half)] = total[:, :, twin * half : (twin + 1) * half]

    mine, xs, ys, corners = [
        [slab_of(plane, block) for plane in plane_at] for block in (b, by_x, by_y, across)
    ]

    def z_in(step, h, when=None):
        def action():
            arrive(mine[step], h)
            send(("z", step), mine[step], b, onward[step], h, goes_on[step])
            send(("s", step), mine[step], sib, z, h)

        guarded(when, action)

    def to_x(step, h, when=None):
        guarded(when, lambda: send(("x", step), mine[step], by_x, z, h))

    def to_y(step, h, when=None):
        guarded(when, lambda: send(("y", step), mine[step], by_y, z, h))

    def xy(step, h, when=None):
        to_x(step, h, when)
        to_y(step, h, when)

    def x_in(step, h):
        arrive(xs[step], h)
        if h == 0 and step in (0, 3):
            send(("xy", step), xs[step], by_y, z, h, at_end if step else None)
        send(("xs", step), xs[step], sib, z, h)

    def y_in(step, h):
        arrive(ys[step], h)
        if h == 1 and step in (0, 3):
            send(("yx", step), ys[step], by_x, z, h, at_end if step else None)
        send(("ys", step), ys[step], sib, z, h)

    def c_in(step, h, when=None):
        def action():
            arrive(corners[step], h)
            if step == 0:
                send(("cu",), corners[step], b, up, h, has_up)
                send(("cd",), corners[step], b, down, h, has_down)
            elif step < 3:
                send(("cz", step), corners[step], b, onward[step], h, in_middle)
            send(("cs", step), corners[step], sib, z, h)

        guarded(when, action)

    for h in range(2):
        whiten_half(h)
        if h == 0:
            pl.semaphore_wait(barrier, 3 + has_up.astype(jnp.int32) + has_down.astype(jnp.int32))
        send(("u",), own, b, up, h, has_up)
        send(("d",), own, b, down, h, has_down)
        send(("x", 0), own, by_x, z, h)
        send(("y", 0), own, by_y, z, h)
        send(("s", 0), own, sib, z, h)
    turn(0)
    multiply(0, "b", 0)
    multiply(0, "b", 1)
    z_in(1, 0)
    z_in(2, 0, in_middle)
    xy(1, 0)
    x_in(0, 0)
    y_in(0, 0)
    y_in(0, 1)
    x_in(0, 1)
    z_in(1, 1)
    z_in(2, 1, in_middle)
    xy(1, 1)
    xy(2, 0, in_middle)
    xy(2, 1, in_middle)
    turn(1)
    multiply(0, "x", 0)
    multiply(0, "y", 0)
    z_in(2, 0, at_end)
    xy(2, 0, at_end)
    z_in(3, 0, in_middle)
    xy(3, 0, in_middle)
    x_in(1, 0)
    y_in(1, 0)
    multiply(0, "x", 1)
    multiply(0, "y", 1)
    multiply(1, "b", 0)
    multiply(1, "b", 1)
    z_in(2, 1, at_end)
    xy(2, 1, at_end)
    z_in(3, 1, in_middle)
    xy(3, 1, in_middle)
    c_in(0, 0)
    c_in(0, 1)
    multiply(1, "x", 0)
    multiply(1, "y", 0)
    turn(2)
    z_in(3, 0, at_end)
    c_in(1, 0, in_middle)
    c_in(2, 0, in_middle)
    x_in(1, 1)
    y_in(1, 1)
    multiply(2, "b", 0)
    multiply(2, "b", 1)
    multiply(0, "c", 0)
    multiply(0, "c", 1)
    z_in(3, 1, at_end)
    to_x(3, 0, at_end)
    to_y(3, 1, at_end)
    to_x(3, 1, at_end)
    to_y(3, 0, at_end)
    c_in(1, 1, in_middle)
    c_in(2, 1, in_middle)
    x_in(2, 0)
    y_in(2, 0)
    turn(3)
    multiply(1, "x", 1)
    multiply(1, "y", 1)
    c_in(1, 0, at_end)
    c_in(3, 0, in_middle)
    x_in(2, 1)
    y_in(2, 1)
    multiply(2, "x", 0)
    multiply(2, "y", 0)
    multiply(3, "b", 0)
    multiply(3, "b", 1)
    c_in(1, 1, at_end)
    c_in(3, 1, in_middle)
    x_in(3, 0)
    y_in(3, 1)
    multiply(2, "x", 1)
    multiply(2, "y", 1)
    multiply(1, "c", 0)
    c_in(2, 0, at_end)
    x_in(3, 1)
    y_in(3, 0)
    multiply(3, "x", 0)
    multiply(3, "y", 1)
    multiply(1, "c", 1)
    multiply(2, "c", 0)
    multiply(3, "x", 1)
    multiply(3, "y", 0)
    c_in(3, 0, at_end)
    c_in(3, 1, at_end)
    c_in(2, 1, at_end)
    multiply(3, "c", 0)
    multiply(3, "c", 1)
    multiply(2, "c", 1)

    for index, slab, block, plane, h, when in sends.values():
        guarded(when, make(index, slab, block, plane, h).wait_send)


def store(done, out_ref, sem):
    copy = pltpu.make_async_copy(done, out_ref, sem)
    copy.start()
    copy.wait()


def kernel_body(records, glitch_mask, fir_taps):
    blocks, planes = lax.axis_size("blk"), lax.axis_size("tm")
    chans, segs, seglen = records.shape
    seg_total = glitch_mask.shape[1]
    lags_dev = LAGS // planes
    depth = segs * 2 * BINS
    bf16 = jnp.bfloat16
    shape = (lags_dev, chans, chans * blocks)
    done = pl.pallas_call(
        kernel,
        out_shape=pltpu.VMEM(shape, bf16),
        in_specs=[pl.BlockSpec(memory_space=pltpu.VMEM)] * 5,
        out_specs=pl.BlockSpec(memory_space=pltpu.VMEM),
        scratch_shapes=[
            pltpu.VMEM((blocks * planes, chans, depth), bf16),
            pltpu.VMEM((planes, lags_dev, chans, depth), bf16),
            pltpu.VMEM((8, lags_dev, chans, chans), jnp.float32),
            pltpu.VMEM((8, 128), jnp.float32),
            pltpu.SemaphoreType.DMA((96,)),
            pltpu.SemaphoreType.DMA((blocks * planes, 2)),
        ],
        compiler_params=pltpu.CompilerParams(
            collective_id=0, has_side_effects=True, vmem_limit_bytes=58 * 1024 * 1024
        ),
        cost_estimate=pl.CostEstimate(
            flops=2 * lags_dev * chans * chans * blocks * planes * depth,
            bytes_accessed=2 * lags_dev * chans * chans * blocks,
            transcendentals=0,
        ),
    )(
        records,
        glitch_mask.T,
        fir_taps[None, :],
        jnp.asarray(dft_thirds(seglen)),
        jnp.asarray(lag_rows(seg_total, seglen)),
    )
    return pl.pallas_call(
        store,
        out_shape=jax.ShapeDtypeStruct(shape, bf16),
        in_specs=[pl.BlockSpec(memory_space=pltpu.VMEM)],
        out_specs=pl.BlockSpec(memory_space=pl.ANY),
        scratch_shapes=[pltpu.SemaphoreType.DMA],
        compiler_params=pltpu.CompilerParams(vmem_limit_bytes=4 * 1024 * 1024),
    )(pltpu.with_memory_space_constraint(done, pltpu.VMEM))


def solution(mesh):
    placed = (P("blk", "tm", None), P("blk", None), P())
    small = mesh.shape["blk"] == 8 and mesh.shape["tm"] == 4
    return jax.shard_map(
        kernel_body if small else gathered_body,
        mesh=mesh,
        in_specs=placed,
        out_specs=P("tm", "blk", None),
        check_vma=False,
    )
```

time: 91.3 us -> 75.5 us (0.83)
  the two profiles are of different devices: /device:TPU:17 before, /device:TPU:1 now
where the time goes in v1:
time: 75.5 us; the launch traced here: 75 us
  Pallas kernels  74.8 us (99%)
    pallas_call x1, Pallas kernels, kernel_body(): pl.pallas_call(kernel, out_shape=pltpu.VMEM(shape, bf16), in_specs=[pl.Bl...  72.8 us
    pallas_call x1, Pallas kernels, kernel_body(): pl.pallas_call(store, out_shape=jax.ShapeDtypeStruct(shape, bf16), in_spe...  2.02 us

profile of v1, /device:TPU:1, one launch (start us, length us, event | category | flops | bytes accessed | tf_op | source)
XLA Modules:
  0.0 75.0 jit_solution(6824593650239993913)
XLA Ops:
  0.0 72.8 %shard_map.55.done = bf16[4,256,2048]{2,1,0:T(8,128)(2,1)S(1)} custom-call(bf16[256,4,512]{2,1,0:T(4,128)(2,1)} %x_ref.1, s32[16,256]{1,0:T(8,128)} %bitcast.2, bf16[1,65]{1,0:T(2,128)(2,1)} %bitcast.3, bf16[512,768]{1,0:T(8,128)(2,1)} %constant.4.clone.dft_ref, f32[2,16,128]{2,1,0:T(8,128)} %constant.5.clone.tab_ref), custom_call_target="tpu_custom_call" | custom-call | flops 17179869184 | bytes 4194304 | tf_op jit(solution)/shard_map/pallas_call | solution.py:439
  72.8 2.0 %shard_map.56 = bf16[4,256,2048]{2,1,0:T(8,128)(2,1)} custom-call(bf16[4,256,2048]{2,1,0:T(8,128)(2,1)S(1)} %shard_map.55.done), custom_call_target="tpu_custom_call" | custom-call | tf_op jit(solution)/shard_map/pallas_call | solution.py:467

commit v2 on v1

--- a/solution.py
+++ b/solution.py
@@ -100,15 +100,38 @@
     )
 
 
+PHASES = (
+    ("0b01", "0b11",),
+    ("0A01", "0B01",),
+    ("0A11", "0B11", "0D00", "0D10",),
+    ("1b01", "1b11", "1Ds1",),
+    ("1As1", "1Bs0", "2A01",),
+    ("2B01", "2D00", "2D11",),
+    ("2b01", "2b11", "2A11",),
+    ("3Ds1",),
+    ("1Dl1", "3Dl1",),
+    ("2B10", "3A01", "3B00", "3A11", "3B10", "1Bl0", "1Al1", "3b01", "3b11",),
+)
+OWN_TURNS = (1, 0, 0, 2, 3, 0, 0, 0, 0, 4)
+NEAR_TURNS = (0, 0, 1, 2, 0, 3, 0, 4, 0, 0)
+JOB_CODES = [
+    int(step) * 32 + "bABD".index(key) * 8 + "01sl".index(h) * 2 + int(waits)
+    for line in PHASES
+    for step, key, h, waits in line
+]
+JOB_STARTS = [sum(len(line) for line in PHASES[:at]) for at in range(len(PHASES) + 1)]
 NEAREST = ((0, 1, 2, 3), (1, 2, 0, 3), (2, 1, 3, 0), (3, 2, 1, 0))
 MESH = pl.DeviceIdType.MESH
 
 
-def kernel(x_ref, use_ref, tap_ref, dft_ref, tab_ref, done, slabs, left, acc, taps, sent, got):
+def kernel(
+    x_ref, use_ref, tap_ref, dft_ref, tab_ref, done,
+    slabs, left, acc, tiles, taps, sent, got, sent_tile, got_tile,
+):
     chans, segs, seglen = x_ref.shape
     width = 2 * BINS
     depth = segs * width
-    lags = left.shape[1]
+    lags = tab_ref.shape[1] // 4
     half = chans // 2
     part_ch = half // 2
     b, z = lax.axis_index("blk"), lax.axis_index("tm")
@@ -119,7 +142,11 @@
     by_x = b + 2 - 4 * at_x
     by_y = b + 4 - 8 * at_y
     across = by_x + 4 - 8 * at_y
+    low = at_x == 0
+    near_a, near_b = jnp.where(low, by_x, by_y), jnp.where(low, by_y, by_x)
+    soon, late = at_x, 1 - at_x
     up, down = z + 1, z - 1
+    partner = z + 1 - 2 * lax.rem(z, 2)
     has_up, has_down = z < 3, z > 0
     in_middle = jnp.logical_and(has_up, has_down)
     at_end = jnp.logical_not(in_middle)
@@ -132,7 +159,8 @@
 
     barrier = pltpu.get_barrier_semaphore()
     for block, plane, when in (
-        (sib, z, None), (by_x, z, None), (by_y, z, None), (b, up, has_up), (b, down, has_down)
+        (sib, z, None), (by_x, z, None), (by_y, z, None), (b, up, has_up), (b, down, has_down),
+        (by_x + 1 - 2 * core, z, None), (by_y + 1 - 2 * core, z, None),
     ):
         guarded(
             when,
@@ -201,32 +229,38 @@
 
     sends = {}
 
+    def half_of(h):
+        return {"s": soon, "l": late}[h] if isinstance(h, str) else h
+
+    def part(h):
+        return pl.ds(h * half if isinstance(h, int) else pl.multiple_of(h * half, half), half)
+
     def make(index, slab, block, plane, h):
-        ref = slabs.at[slab, pl.ds(h * half, half)]
+        ref = slabs.at[slab, part(half_of(h))]
         return pltpu.make_async_remote_copy(
-            src_ref=ref, dst_ref=ref, send_sem=sent.at[index], recv_sem=got.at[slab, h],
+            src_ref=ref, dst_ref=ref, send_sem=sent.at[index], recv_sem=got.at[slab, half_of(h)],
             device_id=(block, plane), device_id_type=MESH,
         )
 
     def send(name, slab, block, plane, h, when=None):
-        name = name + (h,)
-        if name not in sends:
-            sends[name] = (len(sends), slab, block, plane, h, when)
-        guarded(when, lambda: make(*sends[name][:-1]).start())
-
-    def arrive(slab, h):
-        make(0, slab, sib, z, h).wait_recv()
-
-    plane_at, onward, goes_on = [z], [None], [None]
+        if (name, h) not in sends:
+            sends[name, h] = (len(sends), slab, block, plane, h, when)
+        guarded(when, lambda: make(*sends[name, h][:-1]).start())
+
+    def arrive(slab, h, when=None):
+        guarded(when, lambda: make(0, slab, sib, z, h).wait_recv())
+
+    plane_at, onward = [z], [None]
     for step in range(1, 4):
         plane = sum(jnp.where(z == at, NEAREST[at][step], 0) for at in range(4))
-        following = jnp.where(plane > z, z - 1, z + 1)
         plane_at.append(plane)
-        onward.append(following)
-        goes_on.append(jnp.logical_and(following >= 0, following <= 3))
+        onward.append(jnp.where(plane > z, z - 1, z + 1))
+
+    def pick(values, index):
+        return sum(jnp.where(index == at, value, 0) for at, value in enumerate(values))
 
     def turn(step):
-        slab = slab_of(plane_at[step], b)
+        slab = slab_of(pick(plane_at, step), b)
 
         def one(lag, carry):
             row = z * lags + lag
@@ -246,180 +280,207 @@
 
         lax.fori_loop(0, lags, one, 0)
 
-    blocks = {"b": b, "x": by_x, "y": by_y, "c": across}
-    steps_done = {}
-
-    def multiply(step, key, h):
-        block = blocks[key]
-        other = block + 1 - 2 * core
-        arrive(slab_of(plane_at[step], other), h)
-        count = steps_done.get((key, h), 0)
-        steps_done[key, h] = count + 1
-        pair = lax.div(block, 2) * 2
-        right = slabs[pl.ds(slab_of(plane_at[step], pair), 2), h * half : (h + 1) * half]
+    def turn_both(step):
+        slab = slab_of(pick(plane_at, step), near_a)
+
+        def one(lag, carry):
+            row = z * lags + lag
+            cos_row = tab_ref[0, pl.ds(row, 1), :]
+            sin_row = tab_ref[1, pl.ds(row, 1), :]
+            group, place = lax.div(lag, 2), part(lax.rem(lag, 2))
+            for s in range(segs):
+                at = s * width
+                real_part = slabs[slab, part(soon), at : at + BINS].astype(jnp.float32)
+                imag_part = slabs[slab, part(soon), at + BINS : at + width].astype(jnp.float32)
+                cos_real, sin_imag = cos_row * real_part, sin_row * imag_part
+                cos_imag, sin_real = cos_row * imag_part, sin_row * real_part
+                for way, (first, second) in enumerate(
+                    ((cos_real - sin_imag, cos_imag + sin_real), (cos_real + sin_imag, cos_imag - sin_real))
+                ):
+                    to = left.at[4 + step, way * lags // 2 + group, place]
+                    to[:, at : at + BINS] = first.astype(jnp.bfloat16)
+                    to[:, at + BINS : at + width] = second.astype(jnp.bfloat16)
+            return carry
+
+        lax.fori_loop(0, lags, one, 0)
+
+    def pair_of(block):
+        return lax.div(block, 2) * 2
+
+    def job(at, carry):
+        code = pick(JOB_CODES, at)
+        step, key = lax.div(code, 32), lax.rem(lax.div(code, 8), 4)
+        h = pick((0, 1, soon, late), lax.rem(lax.div(code, 2), 4))
+        plane = pick(plane_at, step)
+        block = pick((b, near_a, near_b, near_b), key)
+        arrive(slab_of(plane, block + 1 - 2 * core), h, lax.rem(code, 2) == 1)
+        right = slabs[pl.ds(slab_of(plane, pair_of(block)), 2), part(h)]
         term = lax.dot_general(
-            left[step].reshape(lags * chans, depth),
+            left[step + jnp.where(key == 3, 4, 0)].reshape(lags * chans, depth),
             right.reshape(2 * half, depth),
             (((1,), (1,)), ((), ())),
             preferred_element_type=jnp.float32,
-        ).reshape(lags, chans, 2 * half)
-        at = "bxyc".index(key) * 2 + h
-        if count == 0:
-            acc[at] = term
-        elif count < 3:
-            acc[at] += term
+        )
+        acc[key * 2 + h] += term.reshape(lags, chans, 2 * half)
+        return carry
+
+    def finish(at, carry):
+        key, h = lax.div(at, 2), lax.rem(at, 2)
+        pair = pair_of(pick((b, near_a, near_b), key))
+        total = acc[at].astype(jnp.bfloat16)
+        for other in range(2):
+            first = pl.multiple_of((pair + other) * chans + h * half, half)
+            done[:, :, pl.ds(first, half)] = total[:, :, other * half : (other + 1) * half]
+        return carry
+
+    def clear(at, carry):
+        acc[at] = jnp.zeros(acc.shape[1:], jnp.float32)
+        return carry
+
+    pair_b, pair_across = pair_of(near_b), pair_of(across)
+
+    def spot_of(row_half, block, column_half):
+        column = pl.multiple_of(block * chans + column_half * half, half)
+        return done.at[:, pl.ds(pl.multiple_of(row_half * half, half), half), pl.ds(column, half)]
+
+    def tile_copy(kind, h, t):
+        if kind == 0:
+            block, spot, at = near_a, spot_of(soon, pair_b + t, h), soon * 4 + h * 2 + t
         else:
-            total = (acc[at] + term).astype(jnp.bfloat16)
-            for twin in range(2):
-                first = pl.multiple_of((pair + twin) * chans + h * half, half)
-                done[:, :, pl.ds(first, half)] = total[:, :, twin * half : (twin + 1) * half]
-
-    mine, xs, ys, corners = [
-        [slab_of(plane, block) for plane in plane_at] for block in (b, by_x, by_y, across)
+            block, spot, at = pair_b + t, spot_of(h, near_a, soon), soon * 4 + h * 2 + core
+        return pltpu.make_async_remote_copy(
+            src_ref=tiles.at[kind, h, t], dst_ref=spot, send_sem=sent_tile.at[kind * 4 + h * 2 + t],
+            recv_sem=got_tile.at[at], device_id=(block, z), device_id_type=MESH,
+        )
+
+    def emit(h):
+        total = acc[6 + h].reshape(2, lags, half, 2 * half)
+        for t in range(2):
+            tiles[0, h, t] = total[0, :, :, t * half : (t + 1) * half].astype(jnp.bfloat16)
+        for t in range(2):
+            tile_copy(0, h, t).start()
+        for t in range(2):
+            for lag in range(lags):
+                tiles[1, h, t, lag] = total[1, lag, :, t * half : (t + 1) * half].T.astype(jnp.bfloat16)
+        for t in range(2):
+            tile_copy(1, h, t).start()
+
+    mine, slabs_a, slabs_b = [
+        [slab_of(plane, block) for plane in plane_at] for block in (b, near_a, near_b)
     ]
 
     def z_in(step, h, when=None):
-        def action():
-            arrive(mine[step], h)
-            send(("z", step), mine[step], b, onward[step], h, goes_on[step])
-            send(("s", step), mine[step], sib, z, h)
-
-        guarded(when, action)
-
-    def to_x(step, h, when=None):
-        guarded(when, lambda: send(("x", step), mine[step], by_x, z, h))
-
-    def to_y(step, h, when=None):
-        guarded(when, lambda: send(("y", step), mine[step], by_y, z, h))
-
-    def xy(step, h, when=None):
-        to_x(step, h, when)
-        to_y(step, h, when)
-
-    def x_in(step, h):
-        arrive(xs[step], h)
-        if h == 0 and step in (0, 3):
-            send(("xy", step), xs[step], by_y, z, h, at_end if step else None)
-        send(("xs", step), xs[step], sib, z, h)
-
-    def y_in(step, h):
-        arrive(ys[step], h)
-        if h == 1 and step in (0, 3):
-            send(("yx", step), ys[step], by_x, z, h, at_end if step else None)
-        send(("ys", step), ys[step], sib, z, h)
-
-    def c_in(step, h, when=None):
-        def action():
-            arrive(corners[step], h)
-            if step == 0:
-                send(("cu",), corners[step], b, up, h, has_up)
-                send(("cd",), corners[step], b, down, h, has_down)
-            elif step < 3:
-                send(("cz", step), corners[step], b, onward[step], h, in_middle)
-            send(("cs", step), corners[step], sib, z, h)
-
-        guarded(when, action)
+        arrive(mine[step], h, when)
+        if when is not at_end:
+            send(("on", step), mine[step], b, onward[step], h, in_middle)
+        send(("z", step, when is at_end), mine[step], sib, z, h, when)
+
+    def xy(step, h, when):
+        send(("x", step, when is at_end), mine[step], by_x, z, h, when)
+        send(("y", step, when is at_end), mine[step], by_y, z, h, when)
+
+    def take(key, step, h):
+        slab = (slabs_a if key == "A" else slabs_b)[step]
+        arrive(slab, h)
+        if step == 0:
+            send((key, "p"), slab, b, partner, h, at_end)
+        send((key, step), slab, sib, z, h)
+
+    def land_1():
+        z_in(1, 0)
+        z_in(2, 0, in_middle)
+        xy(1, 0, in_middle)
+        take("A", 0, 0)
+        take("B", 0, 0)
+
+    def land_2():
+        z_in(1, 1)
+        z_in(2, 1, in_middle)
+        send(("x", 1, True), mine[1], by_x, z, "l", at_end)
+        send(("y", 1, True), mine[1], by_y, z, "s", at_end)
+        xy(1, 1, in_middle)
+        take("A", 0, 1)
+        take("B", 0, 1)
+
+    def land_3():
+        z_in(2, 0, at_end)
+        xy(2, 0, at_end)
+        z_in(3, 0, in_middle)
+        xy(3, 0, in_middle)
+        take("A", 1, "s")
+        take("B", 1, "s")
+
+    def land_4():
+        z_in(2, 1, at_end)
+        xy(2, 1, at_end)
+        z_in(3, 1, in_middle)
+        xy(3, 1, in_middle)
+        send(("B", "m"), slabs_b[0], b, partner, "l", in_middle)
+        send(("A", "m"), slabs_a[0], b, partner, "l", in_middle)
+        take("A", 2, 0)
+        take("B", 2, 0)
+
+    def land_5():
+        z_in(3, 0, at_end)
+        xy(3, 0, at_end)
+        take("A", 2, 1)
+        take("B", 2, 1)
+
+    def land_6():
+        z_in(3, 1, at_end)
+        xy(3, 1, at_end)
+        take("A", 3, 0)
+        take("B", 3, 0)
+
+    def land_7():
+        take("A", 3, 1)
+        take("B", 3, 1)
+        take("B", 1, "l")
+
+    def land_9():
+        take("A", 1, "l")
+
+    landings = {1: land_1, 2: land_2, 3: land_3, 4: land_4, 5: land_5, 6: land_6, 7: land_7, 9: land_9}
+
+    def phase(k, carry):
+        for at, land in landings.items():
+            pl.when(k == at)(land)
+        own_step, near_step = pick(OWN_TURNS, k), pick(NEAR_TURNS, k)
+        pl.when(own_step > 0)(lambda: turn(own_step - 1))
+        pl.when(near_step > 0)(lambda: turn_both(near_step - 1))
+        lax.fori_loop(pick(JOB_STARTS, k), pick(JOB_STARTS[1:], k), job, 0)
+        pl.when(jnp.logical_and(k >= 7, k <= 8))(lambda: emit(jnp.where(k == 7, soon, late)))
+        return carry
 
     for h in range(2):
         whiten_half(h)
         if h == 0:
-            pl.semaphore_wait(barrier, 3 + has_up.astype(jnp.int32) + has_down.astype(jnp.int32))
-        send(("u",), own, b, up, h, has_up)
-        send(("d",), own, b, down, h, has_down)
+            pl.semaphore_wait(barrier, 5 + has_up.astype(jnp.int32) + has_down.astype(jnp.int32))
+        send(("up",), own, b, up, h, has_up)
+        send(("down",), own, b, down, h, has_down)
         send(("x", 0), own, by_x, z, h)
         send(("y", 0), own, by_y, z, h)
         send(("s", 0), own, sib, z, h)
-    turn(0)
-    multiply(0, "b", 0)
-    multiply(0, "b", 1)
-    z_in(1, 0)
-    z_in(2, 0, in_middle)
-    xy(1, 0)
-    x_in(0, 0)
-    y_in(0, 0)
-    y_in(0, 1)
-    x_in(0, 1)
-    z_in(1, 1)
-    z_in(2, 1, in_middle)
-    xy(1, 1)
-    xy(2, 0, in_middle)
-    xy(2, 1, in_middle)
-    turn(1)
-    multiply(0, "x", 0)
-    multiply(0, "y", 0)
-    z_in(2, 0, at_end)
-    xy(2, 0, at_end)
-    z_in(3, 0, in_middle)
-    xy(3, 0, in_middle)
-    x_in(1, 0)
-    y_in(1, 0)
-    multiply(0, "x", 1)
-    multiply(0, "y", 1)
-    multiply(1, "b", 0)
-    multiply(1, "b", 1)
-    z_in(2, 1, at_end)
-    xy(2, 1, at_end)
-    z_in(3, 1, in_middle)
-    xy(3, 1, in_middle)
-    c_in(0, 0)
-    c_in(0, 1)
-    multiply(1, "x", 0)
-    multiply(1, "y", 0)
-    turn(2)
-    z_in(3, 0, at_end)
-    c_in(1, 0, in_middle)
-    c_in(2, 0, in_middle)
-    x_in(1, 1)
-    y_in(1, 1)
-    multiply(2, "b", 0)
-    multiply(2, "b", 1)
-    multiply(0, "c", 0)
-    multiply(0, "c", 1)
-    z_in(3, 1, at_end)
-    to_x(3, 0, at_end)
-    to_y(3, 1, at_end)
-    to_x(3, 1, at_end)
-    to_y(3, 0, at_end)
-    c_in(1, 1, in_middle)
-    c_in(2, 1, in_middle)
-    x_in(2, 0)
-    y_in(2, 0)
-    turn(3)
-    multiply(1, "x", 1)
-    multiply(1, "y", 1)
-    c_in(1, 0, at_end)
-    c_in(3, 0, in_middle)
-    x_in(2, 1)
-    y_in(2, 1)
-    multiply(2, "x", 0)
-    multiply(2, "y", 0)
-    multiply(3, "b", 0)
-    multiply(3, "b", 1)
-    c_in(1, 1, at_end)
-    c_in(3, 1, in_middle)
-    x_in(3, 0)
-    y_in(3, 1)
-    multiply(2, "x", 1)
-    multiply(2, "y", 1)
-    multiply(1, "c", 0)
-    c_in(2, 0, at_end)
-    x_in(3, 1)
-    y_in(3, 0)
-    multiply(3, "x", 0)
-    multiply(3, "y", 1)
-    multiply(1, "c", 1)
-    multiply(2, "c", 0)
-    multiply(3, "x", 1)
-    multiply(3, "y", 0)
-    c_in(3, 0, at_end)
-    c_in(3, 1, at_end)
-    c_in(2, 1, at_end)
-    multiply(3, "c", 0)
-    multiply(3, "c", 1)
-    multiply(2, "c", 1)
-
+    lax.fori_loop(0, acc.shape[0], clear, 0)
+    lax.fori_loop(0, len(OWN_TURNS), phase, 0)
+    lax.fori_loop(0, 6, finish, 0)
+
+    for side in range(2):
+        for h in range(2):
+            for t in range(2):
+                spot = spot_of(
+                    jnp.where(low, h, side), pair_across + t, jnp.where(low, side, h)
+                )
+                pltpu.make_async_remote_copy(
+                    src_ref=tiles.at[0, 0, 0], dst_ref=spot, send_sem=sent_tile.at[0],
+                    recv_sem=got_tile.at[side * 4 + h * 2 + t], device_id=(sib, z), device_id_type=MESH,
+                ).wait_recv()
     for index, slab, block, plane, h, when in sends.values():
         guarded(when, make(index, slab, block, plane, h).wait_send)
+    for kind in range(2):
+        for h in range(2):
+            for t in range(2):
+                tile_copy(kind, h, t).wait_send()
 
 
 def store(done, out_ref, sem):
@@ -434,6 +495,7 @@
     seg_total = glitch_mask.shape[1]
     lags_dev = LAGS // planes
     depth = segs * 2 * BINS
+    half = chans // 2
     bf16 = jnp.bfloat16
     shape = (lags_dev, chans, chans * blocks)
     done = pl.pallas_call(
@@ -443,11 +505,14 @@
         out_specs=pl.BlockSpec(memory_space=pltpu.VMEM),
         scratch_shapes=[
             pltpu.VMEM((blocks * planes, chans, depth), bf16),
-            pltpu.VMEM((planes, lags_dev, chans, depth), bf16),
+            pltpu.VMEM((2 * planes, lags_dev, chans, depth), bf16),
             pltpu.VMEM((8, lags_dev, chans, chans), jnp.float32),
+            pltpu.VMEM((2, 2, 2, lags_dev, half, half), bf16),
             pltpu.VMEM((8, 128), jnp.float32),
             pltpu.SemaphoreType.DMA((96,)),
             pltpu.SemaphoreType.DMA((blocks * planes, 2)),
+            pltpu.SemaphoreType.DMA((8,)),
+            pltpu.SemaphoreType.DMA((8,)),
         ],
         compiler_params=pltpu.CompilerParams(
             collective_id=0, has_side_effects=True, vmem_limit_bytes=58 * 1024 * 1024

time: 75.5 us -> 68.1 us (0.902)
  Pallas kernels: 74.8 us -> 68 us
    pallas_call x1, Pallas kernels: 72.8 us -> 65.9 us  [kernel_body(): pl.pallas_call(kernel, out_shape=pltpu.VMEM(shape, bf16), in_specs=[pl.Bl...]
where the time goes in v2:
time: 68.1 us; the launch traced here: 68 us
  Pallas kernels  68 us (100%)
    pallas_call x1, Pallas kernels, kernel_body(): pl.pallas_call(kernel, out_shape=pltpu.VMEM(shape, bf16), in_specs=[pl.Bl...  65.9 us
    pallas_call x1, Pallas kernels, kernel_body(): pl.pallas_call(store, out_shape=jax.ShapeDtypeStruct(shape, bf16), in_spe...  2.02 us

profile of v2, /device:TPU:1, one launch (start us, length us, event | category | flops | bytes accessed | tf_op | source)
XLA Modules:
  0.0 68.0 jit_solution(17627727408548174811)
XLA Ops:
  0.0 65.9 %shard_map.55.done = bf16[4,256,2048]{2,1,0:T(8,128)(2,1)S(1)} custom-call(bf16[256,4,512]{2,1,0:T(4,128)(2,1)} %x_ref.1, s32[16,256]{1,0:T(8,128)} %bitcast.2, bf16[1,65]{1,0:T(2,128)(2,1)} %bitcast.3, bf16[512,768]{1,0:T(8,128)(2,1)} %constant.4.clone.dft_ref, f32[2,16,128]{2,1,0:T(8,128)} %constant.5.clone.tab_ref), custom_call_target="tpu_custom_call" | custom-call | flops 17179869184 | bytes 4194304 | tf_op jit(solution)/shard_map/pallas_call | solution.py:501
  66.0 2.0 %shard_map.56 = bf16[4,256,2048]{2,1,0:T(8,128)(2,1)} custom-call(bf16[4,256,2048]{2,1,0:T(8,128)(2,1)S(1)} %shard_map.55.done), custom_call_target="tpu_custom_call" | custom-call | tf_op jit(solution)/shard_map/pallas_call | solution.py:532

commit v3 on v2

--- a/solution.py
+++ b/solution.py
@@ -100,26 +100,47 @@
     )
 
 
-PHASES = (
+END_PHASES = (
     ("0b01", "0b11",),
     ("0A01", "0B01",),
     ("0A11", "0B11", "0D00", "0D10",),
-    ("1b01", "1b11", "1Ds1",),
-    ("1As1", "1Bs0", "2A01",),
+    ("1b01", "1b11", "1D01",),
+    ("1As1", "1B00", "2A01",),
     ("2B01", "2D00", "2D11",),
-    ("2b01", "2b11", "2A11",),
-    ("3Ds1",),
-    ("1Dl1", "3Dl1",),
-    ("2B10", "3A01", "3B00", "3A11", "3B10", "1Bl0", "1Al1", "3b01", "3b11",),
+    ("2b01", "2b11", "2A11", "2B10",),
+    ("3D01",),
+    ("1D11", "3D11",),
+    ("3A01", "3B00", "3A11", "3B10", "1B10", "1Al1", "3b01", "3b11",),
 )
-OWN_TURNS = (1, 0, 0, 2, 3, 0, 0, 0, 0, 4)
+MIDDLE_PHASES = (
+    ("0b01", "0b11",),
+    ("0A01", "0B01",),
+    ("0A11", "0B11", "0D00", "0D10",),
+    ("1b01", "1b11", "1D01",),
+    ("1As1", "1B00", "2A01",),
+    ("2B01", "2D00", "2b01", "2b11",),
+    ("2D11",),
+    ("3D01",),
+    ("1D11", "3D11",),
+    ("2A11", "2B10", "3A01", "3B00", "3A11", "3B10", "1B10", "1Al1", "3b01", "3b11",),
+)
+END_TURNS = (1, 0, 0, 2, 3, 0, 4, 0, 0, 0)
+MIDDLE_TURNS = (1, 0, 0, 2, 3, 0, 0, 0, 0, 4)
 NEAR_TURNS = (0, 0, 1, 2, 0, 3, 0, 4, 0, 0)
-JOB_CODES = [
-    int(step) * 32 + "bABD".index(key) * 8 + "01sl".index(h) * 2 + int(waits)
-    for line in PHASES
-    for step, key, h, waits in line
-]
-JOB_STARTS = [sum(len(line) for line in PHASES[:at]) for at in range(len(PHASES) + 1)]
+
+
+def job_codes(phases):
+    return [
+        int(step) * 32 + "bABD".index(key) * 8 + "01sl".index(h) * 2 + int(waits)
+        for line in phases
+        for step, key, h, waits in line
+    ]
+
+
+def job_starts(phases):
+    return [sum(len(line) for line in phases[:at]) for at in range(len(phases) + 1)]
+
+
 NEAREST = ((0, 1, 2, 3), (1, 2, 0, 3), (2, 1, 3, 0), (3, 2, 1, 0))
 MESH = pl.DeviceIdType.MESH
 
@@ -142,7 +163,7 @@
     by_x = b + 2 - 4 * at_x
     by_y = b + 4 - 8 * at_y
     across = by_x + 4 - 8 * at_y
-    low = at_x == 0
+    low, high = at_x == 0, at_x == 1
     near_a, near_b = jnp.where(low, by_x, by_y), jnp.where(low, by_y, by_x)
     soon, late = at_x, 1 - at_x
     up, down = z + 1, z - 1
@@ -307,8 +328,17 @@
     def pair_of(block):
         return lax.div(block, 2) * 2
 
+    def by_place(end, middle):
+        return [
+            one if one == two else jnp.where(in_middle, two, one) for one, two in zip(end, middle)
+        ]
+
+    codes = by_place(job_codes(END_PHASES), job_codes(MIDDLE_PHASES))
+    starts = by_place(job_starts(END_PHASES), job_starts(MIDDLE_PHASES))
+    own_turns = by_place(END_TURNS, MIDDLE_TURNS)
+
     def job(at, carry):
-        code = pick(JOB_CODES, at)
+        code = pick(codes, at)
         step, key = lax.div(code, 32), lax.rem(lax.div(code, 8), 4)
         h = pick((0, 1, soon, late), lax.rem(lax.div(code, 2), 4))
         plane = pick(plane_at, step)
@@ -362,7 +392,6 @@
         for t in range(2):
             for lag in range(lags):
                 tiles[1, h, t, lag] = total[1, lag, :, t * half : (t + 1) * half].T.astype(jnp.bfloat16)
-        for t in range(2):
             tile_copy(1, h, t).start()
 
     mine, slabs_a, slabs_b = [
@@ -379,12 +408,12 @@
         send(("x", step, when is at_end), mine[step], by_x, z, h, when)
         send(("y", step, when is at_end), mine[step], by_y, z, h, when)
 
-    def take(key, step, h):
+    def take(key, step, h, when=None):
         slab = (slabs_a if key == "A" else slabs_b)[step]
-        arrive(slab, h)
+        arrive(slab, h, when)
         if step == 0:
             send((key, "p"), slab, b, partner, h, at_end)
-        send((key, step), slab, sib, z, h)
+        send((key, step, when is at_end, when is low), slab, sib, z, h, when)
 
     def land_1():
         z_in(1, 0)
@@ -396,7 +425,7 @@
     def land_2():
         z_in(1, 1)
         z_in(2, 1, in_middle)
-        send(("x", 1, True), mine[1], by_x, z, "l", at_end)
+        send(("x", 1, True), mine[1], by_x, z, 0, at_end)
         send(("y", 1, True), mine[1], by_y, z, "s", at_end)
         xy(1, 1, in_middle)
         take("A", 0, 1)
@@ -408,14 +437,14 @@
         z_in(3, 0, in_middle)
         xy(3, 0, in_middle)
         take("A", 1, "s")
-        take("B", 1, "s")
+        take("B", 1, 0)
 
     def land_4():
         z_in(2, 1, at_end)
         xy(2, 1, at_end)
         z_in(3, 1, in_middle)
         xy(3, 1, in_middle)
-        send(("B", "m"), slabs_b[0], b, partner, "l", in_middle)
+        send(("B", "m"), slabs_b[0], b, partner, 1, in_middle)
         send(("A", "m"), slabs_a[0], b, partner, "l", in_middle)
         take("A", 2, 0)
         take("B", 2, 0)
@@ -424,32 +453,36 @@
         z_in(3, 0, at_end)
         xy(3, 0, at_end)
         take("A", 2, 1)
-        take("B", 2, 1)
+        take("B", 2, 1, at_end)
 
     def land_6():
         z_in(3, 1, at_end)
         xy(3, 1, at_end)
         take("A", 3, 0)
         take("B", 3, 0)
+        take("B", 2, 1, in_middle)
 
     def land_7():
-        take("A", 3, 1)
+        take("A", 3, 1, high)
+
+    def land_8():
+        take("A", 3, 1, low)
         take("B", 3, 1)
-        take("B", 1, "l")
+        take("B", 1, 1)
 
     def land_9():
         take("A", 1, "l")
 
-    landings = {1: land_1, 2: land_2, 3: land_3, 4: land_4, 5: land_5, 6: land_6, 7: land_7, 9: land_9}
+    landings = {1: land_1, 2: land_2, 3: land_3, 4: land_4, 5: land_5, 6: land_6, 7: land_7, 8: land_8, 9: land_9}
 
     def phase(k, carry):
         for at, land in landings.items():
             pl.when(k == at)(land)
-        own_step, near_step = pick(OWN_TURNS, k), pick(NEAR_TURNS, k)
+        own_step, near_step = pick(own_turns, k), pick(NEAR_TURNS, k)
         pl.when(own_step > 0)(lambda: turn(own_step - 1))
         pl.when(near_step > 0)(lambda: turn_both(near_step - 1))
-        lax.fori_loop(pick(JOB_STARTS, k), pick(JOB_STARTS[1:], k), job, 0)
-        pl.when(jnp.logical_and(k >= 7, k <= 8))(lambda: emit(jnp.where(k == 7, soon, late)))
+        lax.fori_loop(pick(starts, k), pick(starts[1:], k), job, 0)
+        pl.when(jnp.logical_and(k >= 7, k <= 8))(lambda: emit(k - 7))
         return carry
 
     for h in range(2):
@@ -462,7 +495,7 @@
         send(("y", 0), own, by_y, z, h)
         send(("s", 0), own, sib, z, h)
     lax.fori_loop(0, acc.shape[0], clear, 0)
-    lax.fori_loop(0, len(OWN_TURNS), phase, 0)
+    lax.fori_loop(0, len(END_TURNS), phase, 0)
     lax.fori_loop(0, 6, finish, 0)
 
     for side in range(2):
@@ -484,9 +517,13 @@
 
 
 def store(done, out_ref, sem):
-    copy = pltpu.make_async_copy(done, out_ref, sem)
-    copy.start()
-    copy.wait()
+    copies = [
+        pltpu.make_async_copy(done.at[lag], out_ref.at[lag], sem.at[lag]) for lag in range(done.shape[0])
+    ]
+    for copy in copies:
+        copy.start()
+    for copy in copies:
+        copy.wait()
 
 
 def kernel_body(records, glitch_mask, fir_taps):
@@ -534,7 +571,7 @@
         out_shape=jax.ShapeDtypeStruct(shape, bf16),
         in_specs=[pl.BlockSpec(memory_space=pltpu.VMEM)],
         out_specs=pl.BlockSpec(memory_space=pl.ANY),
-        scratch_shapes=[pltpu.SemaphoreType.DMA],
+        scratch_shapes=[pltpu.SemaphoreType.DMA((lags_dev,))],
         compiler_params=pltpu.CompilerParams(vmem_limit_bytes=4 * 1024 * 1024),
     )(pltpu.with_memory_space_constraint(done, pltpu.VMEM))
 

time: 68.1 us -> 66 us (0.969)
  Pallas kernels: 68 us -> 65.8 us
    pallas_call x1, Pallas kernels: 65.9 us -> 63.8 us  [kernel_body(): pl.pallas_call(kernel, out_shape=pltpu.VMEM(shape, bf16), in_specs=[pl.Bl...]
where the time goes in v3:
time: 66 us; the launch traced here: 65.8 us
  Pallas kernels  65.8 us (100%)
    pallas_call x1, Pallas kernels, kernel_body(): pl.pallas_call(kernel, out_shape=pltpu.VMEM(shape, bf16), in_specs=[pl.Bl...  63.8 us
    pallas_call x1, Pallas kernels, kernel_body(): pl.pallas_call(store, out_shape=jax.ShapeDtypeStruct(shape, bf16), in_spe...  2.04 us

profile of v3, /device:TPU:1, one launch (start us, length us, event | category | flops | bytes accessed | tf_op | source)
XLA Modules:
  0.0 65.8 jit_solution(10317269453985708672)
XLA Ops:
  0.0 63.8 %shard_map.55.done = bf16[4,256,2048]{2,1,0:T(8,128)(2,1)S(1)} custom-call(bf16[256,4,512]{2,1,0:T(4,128)(2,1)} %x_ref.1, s32[16,256]{1,0:T(8,128)} %bitcast.2, bf16[1,65]{1,0:T(2,128)(2,1)} %bitcast.3, bf16[512,768]{1,0:T(8,128)(2,1)} %constant.4.clone.dft_ref, f32[2,16,128]{2,1,0:T(8,128)} %constant.5.clone.tab_ref), custom_call_target="tpu_custom_call" | custom-call | flops 17179869184 | bytes 4194304 | tf_op jit(solution)/shard_map/pallas_call | solution.py:538
  63.8 2.0 %shard_map.56 = bf16[4,256,2048]{2,1,0:T(8,128)(2,1)} custom-call(bf16[4,256,2048]{2,1,0:T(8,128)(2,1)S(1)} %shard_map.55.done), custom_call_target="tpu_custom_call" | custom-call | tf_op jit(solution)/shard_map/pallas_call | solution.py:569

commit v4 on v3

--- a/solution.py
+++ b/solution.py
@@ -106,11 +106,11 @@
     ("0A11", "0B11", "0D00", "0D10",),
     ("1b01", "1b11", "1D01",),
     ("1As1", "1B00", "2A01",),
-    ("2B01", "2D00", "2D11",),
-    ("2b01", "2b11", "2A11", "2B10",),
+    ("2B01", "2D00", "2D11", "2b01",),
+    ("2b11", "2A11", "2B10",),
     ("3D01",),
-    ("1D11", "3D11",),
-    ("3A01", "3B00", "3A11", "3B10", "1B10", "1Al1", "3b01", "3b11",),
+    ("3A01", "3D11", "1D11",),
+    ("3B00", "3A11", "3B10", "1B10", "1Al1", "3b01", "3b11",),
 )
 MIDDLE_PHASES = (
     ("0b01", "0b11",),
@@ -121,11 +121,11 @@
     ("2B01", "2D00", "2b01", "2b11",),
     ("2D11",),
     ("3D01",),
-    ("1D11", "3D11",),
-    ("2A11", "2B10", "3A01", "3B00", "3A11", "3B10", "1B10", "1Al1", "3b01", "3b11",),
+    ("3A01", "3D11", "1D11",),
+    ("2A11", "2B10", "3B00", "3A11", "3B10", "1B10", "1Al1", "3b01", "3b11",),
 )
 END_TURNS = (1, 0, 0, 2, 3, 0, 4, 0, 0, 0)
-MIDDLE_TURNS = (1, 0, 0, 2, 3, 0, 0, 0, 0, 4)
+MIDDLE_TURNS = (1, 0, 0, 2, 3, 0, 0, 0, 4, 0)
 NEAR_TURNS = (0, 0, 1, 2, 0, 3, 0, 4, 0, 0)
 
 
@@ -280,50 +280,48 @@
     def pick(values, index):
         return sum(jnp.where(index == at, value, 0) for at, value in enumerate(values))
 
+    def rows_of(at):
+        lag, s = lax.div(at, segs), lax.rem(at, segs)
+        row = z * lags + lag
+        first = pl.multiple_of(s * width, width)
+        return lag, tab_ref[0, pl.ds(row, 1), :], tab_ref[1, pl.ds(row, 1), :], first
+
     def turn(step):
         slab = slab_of(pick(plane_at, step), b)
 
-        def one(lag, carry):
-            row = z * lags + lag
-            cos_row = tab_ref[0, pl.ds(row, 1), :]
-            sin_row = tab_ref[1, pl.ds(row, 1), :]
-            for s in range(segs):
-                at = s * width
-                real_part = slabs[slab, :, at : at + BINS].astype(jnp.float32)
-                imag_part = slabs[slab, :, at + BINS : at + width].astype(jnp.float32)
-                left[step, lag, :, at : at + BINS] = (
-                    cos_row * real_part - sin_row * imag_part
-                ).astype(jnp.bfloat16)
-                left[step, lag, :, at + BINS : at + width] = (
-                    cos_row * imag_part + sin_row * real_part
-                ).astype(jnp.bfloat16)
+        def one(at, carry):
+            lag, cos_row, sin_row, first = rows_of(at)
+            real_part = slabs[slab, :, pl.ds(first, BINS)].astype(jnp.float32)
+            imag_part = slabs[slab, :, pl.ds(first + BINS, BINS)].astype(jnp.float32)
+            left[step, lag, :, pl.ds(first, BINS)] = (
+                cos_row * real_part - sin_row * imag_part
+            ).astype(jnp.bfloat16)
+            left[step, lag, :, pl.ds(first + BINS, BINS)] = (
+                cos_row * imag_part + sin_row * real_part
+            ).astype(jnp.bfloat16)
             return carry
 
-        lax.fori_loop(0, lags, one, 0)
+        lax.fori_loop(0, lags * segs, one, 0)
 
     def turn_both(step):
         slab = slab_of(pick(plane_at, step), near_a)
 
-        def one(lag, carry):
-            row = z * lags + lag
-            cos_row = tab_ref[0, pl.ds(row, 1), :]
-            sin_row = tab_ref[1, pl.ds(row, 1), :]
+        def one(at, carry):
+            lag, cos_row, sin_row, first = rows_of(at)
             group, place = lax.div(lag, 2), part(lax.rem(lag, 2))
-            for s in range(segs):
-                at = s * width
-                real_part = slabs[slab, part(soon), at : at + BINS].astype(jnp.float32)
-                imag_part = slabs[slab, part(soon), at + BINS : at + width].astype(jnp.float32)
-                cos_real, sin_imag = cos_row * real_part, sin_row * imag_part
-                cos_imag, sin_real = cos_row * imag_part, sin_row * real_part
-                for way, (first, second) in enumerate(
-                    ((cos_real - sin_imag, cos_imag + sin_real), (cos_real + sin_imag, cos_imag - sin_real))
-                ):
-                    to = left.at[4 + step, way * lags // 2 + group, place]
-                    to[:, at : at + BINS] = first.astype(jnp.bfloat16)
-                    to[:, at + BINS : at + width] = second.astype(jnp.bfloat16)
+            real_part = slabs[slab, part(soon), pl.ds(first, BINS)].astype(jnp.float32)
+            imag_part = slabs[slab, part(soon), pl.ds(first + BINS, BINS)].astype(jnp.float32)
+            cos_real, sin_imag = cos_row * real_part, sin_row * imag_part
+            cos_imag, sin_real = cos_row * imag_part, sin_row * real_part
+            for way, (one_part, two_part) in enumerate(
+                ((cos_real - sin_imag, cos_imag + sin_real), (cos_real + sin_imag, cos_imag - sin_real))
+            ):
+                to = left.at[4 + step, way * lags // 2 + group, place]
+                to[:, pl.ds(first, BINS)] = one_part.astype(jnp.bfloat16)
+                to[:, pl.ds(first + BINS, BINS)] = two_part.astype(jnp.bfloat16)
             return carry
 
-        lax.fori_loop(0, lags, one, 0)
+        lax.fori_loop(0, lags * segs, one, 0)
 
     def pair_of(block):
         return lax.div(block, 2) * 2
@@ -466,9 +464,9 @@
         take("A", 3, 1, high)
 
     def land_8():
-        take("A", 3, 1, low)
         take("B", 3, 1)
         take("B", 1, 1)
+        take("A", 3, 1, low)
 
     def land_9():
         take("A", 1, "l")

time: 66 us -> 65.8 us (level)
  no operation moved by 1% of the time
where the time goes in v4:
time: 65.8 us; the launch traced here: 65.6 us
  Pallas kernels  65.6 us (100%)
    pallas_call x1, Pallas kernels, kernel_body(): pl.pallas_call(kernel, out_shape=pltpu.VMEM(shape, bf16), in_specs=[pl.Bl...  63.6 us
    pallas_call x1, Pallas kernels, kernel_body(): pl.pallas_call(store, out_shape=jax.ShapeDtypeStruct(shape, bf16), in_spe...  2.04 us

profile of v4, /device:TPU:1, one launch (start us, length us, event | category | flops | bytes accessed | tf_op | source)
XLA Modules:
  0.0 65.6 jit_solution(11161895698776945413)
XLA Ops:
  0.0 63.6 %shard_map.55.done = bf16[4,256,2048]{2,1,0:T(8,128)(2,1)S(1)} custom-call(bf16[256,4,512]{2,1,0:T(4,128)(2,1)} %x_ref.1, s32[16,256]{1,0:T(8,128)} %bitcast.2, bf16[1,65]{1,0:T(2,128)(2,1)} %bitcast.3, bf16[512,768]{1,0:T(8,128)(2,1)} %constant.4.clone.dft_ref, f32[2,16,128]{2,1,0:T(8,128)} %constant.5.clone.tab_ref), custom_call_target="tpu_custom_call" | custom-call | flops 17179869184 | bytes 4194304 | tf_op jit(solution)/shard_map/pallas_call | solution.py:536
  63.6 2.0 %shard_map.56 = bf16[4,256,2048]{2,1,0:T(8,128)(2,1)} custom-call(bf16[4,256,2048]{2,1,0:T(8,128)(2,1)S(1)} %shard_map.55.done), custom_call_target="tpu_custom_call" | custom-call | tf_op jit(solution)/shard_map/pallas_call | solution.py:567

commit v5 on v4

--- a/solution.py
+++ b/solution.py
@@ -496,6 +496,8 @@
     lax.fori_loop(0, len(END_TURNS), phase, 0)
     lax.fori_loop(0, 6, finish, 0)
 
+    for index, slab, block, plane, h, when in sends.values():
+        guarded(when, make(index, slab, block, plane, h).wait_send)
     for side in range(2):
         for h in range(2):
             for t in range(2):
@@ -506,8 +508,6 @@
                     src_ref=tiles.at[0, 0, 0], dst_ref=spot, send_sem=sent_tile.at[0],
                     recv_sem=got_tile.at[side * 4 + h * 2 + t], device_id=(sib, z), device_id_type=MESH,
                 ).wait_recv()
-    for index, slab, block, plane, h, when in sends.values():
-        guarded(when, make(index, slab, block, plane, h).wait_send)
     for kind in range(2):
         for h in range(2):
             for t in range(2):

time: 65.8 us -> 65.7 us (level)
  no operation moved by 1% of the time
where the time goes in v5:
time: 65.7 us; the launch traced here: 65.6 us
  Pallas kernels  65.5 us (100%)
    pallas_call x1, Pallas kernels, kernel_body(): pl.pallas_call(kernel, out_shape=pltpu.VMEM(shape, bf16), in_specs=[pl.Bl...  63.5 us
    pallas_call x1, Pallas kernels, kernel_body(): pl.pallas_call(store, out_shape=jax.ShapeDtypeStruct(shape, bf16), in_spe...  2.04 us

profile of v5, /device:TPU:1, one launch (start us, length us, event | category | flops | bytes accessed | tf_op | source)
XLA Modules:
  0.0 65.6 jit_solution(9918293441463844851)
XLA Ops:
  0.0 63.5 %shard_map.55.done = bf16[4,256,2048]{2,1,0:T(8,128)(2,1)S(1)} custom-call(bf16[256,4,512]{2,1,0:T(4,128)(2,1)} %x_ref.1, s32[16,256]{1,0:T(8,128)} %bitcast.2, bf16[1,65]{1,0:T(2,128)(2,1)} %bitcast.3, bf16[512,768]{1,0:T(8,128)(2,1)} %constant.4.clone.dft_ref, f32[2,16,128]{2,1,0:T(8,128)} %constant.5.clone.tab_ref), custom_call_target="tpu_custom_call" | custom-call | flops 17179869184 | bytes 4194304 | tf_op jit(solution)/shard_map/pallas_call | solution.py:536
  63.5 2.0 %shard_map.56 = bf16[4,256,2048]{2,1,0:T(8,128)(2,1)} custom-call(bf16[4,256,2048]{2,1,0:T(8,128)(2,1)S(1)} %shard_map.55.done), custom_call_target="tpu_custom_call" | custom-call | tf_op jit(solution)/shard_map/pallas_call | solution.py:567
